TPU v7x, 128 devices: a whole 4x4x4 slice. The times are simulated.
128 devices in a mesh: slot: 32 (over x, y, core), ulysses: 4 (over z).
Axes of the slice: x: 4, y: 4, z: 4, core: 2. Of those that a mesh axis runs over, the one named last changes fastest.
Arguments:
- queries: bfloat16 [32768, 3072], P(('slot', 'ulysses')), may hold values from -6 to 6
- key_states: bfloat16 [32768, 3072], P(('slot', 'ulysses')), may hold values from -6 to 6
- value_states: bfloat16 [32768, 3072], P(('slot', 'ulysses')), may hold values from -3.5 to 3.5
- query_gain: float32 [128], replicated, may hold values from 0.1 to 1.9
- key_gain: float32 [128], replicated, may hold values from 0.1 to 1.9
- level_gate: float32 [16, 3072], replicated, may hold values from 0.3 to 1.5
- levels: int32 [32], replicated, may hold values from 0 to 15
- lengths: int32 [32], replicated, may hold values from 512 to 1024, as said below
- context: int32 [32], replicated, may hold values from 0 to 3, as said below
Outputs:
- gated: bfloat16 [32768, 3072], P(('slot', 'ulysses'))
Inputs may be any that keep to these rules, and one draw needn't show every extreme that they name: `lengths`: each group uses at least 512 of its token slots; some group uses all 1024. `context`: group c attends to at most c earlier groups; some group attends to 3.
All inputs are finite; a program needn't handle non-finite values.
Results may differ from a plain program's by a relative error of at most 0.0051.
Values may be sent and summed in bfloat16 or wider, within the bound.
A program may use at most 128 MiB of HBM per device.

v0:
```python
import math

import jax
import jax.numpy as jnp
from jax import lax
from jax.sharding import PartitionSpec as P

HD = 128
CTX = 3


def from_behind(block, axis, distance):
    devices = range(lax.axis_size(axis))
    route = [(i - distance, i) for i in devices if i - distance in devices]
    return lax.ppermute(block, axis, route)


def head_norm(states, gain):
    full = states.astype(jnp.float32).reshape(states.shape[0], -1, HD)
    square = jnp.mean(full * full, axis=-1, keepdims=True)
    normed = full * lax.rsqrt(square + 1e-06) * gain
    return normed.reshape(states.shape[0], -1).astype(jnp.bfloat16)


def select_entry(table, position):
    places = jnp.arange(table.shape[0], dtype=jnp.int32)
    return jnp.sum(jnp.where(places == position, table, 0))


def shards(
    queries, key_states, value_states, query_gain, key_gain, level_gate, levels, lengths, context
):
    q_norm = head_norm(queries, query_gain)
    k_norm = head_norm(key_states, key_gain)
    q_heads, k_heads, v_heads = (
        lax.all_to_all(q_norm, "ulysses", split_axis=1, concat_axis=0, tiled=True),
        lax.all_to_all(k_norm, "ulysses", split_axis=1, concat_axis=0, tiled=True),
        lax.all_to_all(value_states, "ulysses", split_axis=1, concat_axis=0, tiled=True),
    )
    group_index = lax.axis_index("slot")
    span_rows = q_heads.shape[0]
    width_here = q_heads.shape[1]
    local_heads = width_here // HD
    own_block = jnp.stack([k_heads, v_heads])
    blocks = [own_block]
    previous = own_block
    for offset in range(1, CTX + 1):
        previous = from_behind(previous, "slot", 1)
        blocks.append(previous)
    reach = select_entry(context, group_index)
    key_rows = jnp.arange(span_rows, dtype=jnp.int32)
    factor = 1.0 / math.sqrt(HD)
    masks = []
    for offset in range(CTX + 1):
        source = jnp.maximum(group_index - offset, 0)
        source_length = select_entry(lengths, source)
        masks.append((offset <= reach) & (key_rows < source_length))

    def one_head(head):
        start = head * HD
        query_block = lax.dynamic_slice_in_dim(q_heads, start, HD, 1)
        weighted = jnp.zeros((span_rows, HD), jnp.float32)
        total = jnp.zeros((span_rows,), jnp.float32)
        for offset in range(CTX + 1):
            key_block = lax.dynamic_slice_in_dim(blocks[offset][0], start, HD, 1)
            value_block = lax.dynamic_slice_in_dim(blocks[offset][1], start, HD, 1)
            scores = (
                lax.dot_general(
                    query_block,
                    key_block,
                    (((1,), (1,)), ((), ())),
                    preferred_element_type=jnp.float32,
                )
                * factor
            )
            weight = jnp.where(masks[offset][None, :], jnp.exp(scores), 0.0)
            total = total + jnp.sum(weight, axis=-1)
            weighted = weighted + jnp.dot(
                weight.astype(jnp.bfloat16), value_block, preferred_element_type=jnp.float32
            )
        return weighted / total[:, None]

    per_head = lax.map(one_head, jnp.arange(local_heads, dtype=jnp.int32))
    attended = jnp.transpose(per_head, (1, 0, 2)).reshape(span_rows, width_here)
    own_length = select_entry(lengths, group_index)
    attended = jnp.where((key_rows < own_length)[:, None], attended, 0.0).astype(jnp.bfloat16)
    restored = lax.all_to_all(attended, "ulysses", split_axis=0, concat_axis=1, tiled=True)
    level_here = select_entry(levels, group_index)
    level_index = jnp.arange(level_gate.shape[0], dtype=jnp.int32)
    gate_row = jnp.sum(jnp.where((level_index == level_here)[:, None], level_gate, 0.0), axis=0)
    return (gate_row[None, :] * restored.astype(jnp.float32)).astype(jnp.bfloat16)


def solution(mesh):
    in_specs = (
        P(("slot", "ulysses"), None),
        P(("slot", "ulysses"), None),
        P(("slot", "ulysses"), None),
        P(),
        P(),
        P(),
        P(),
        P(),
        P(),
    )
    out_specs = P(("slot", "ulysses"), None)
    return jax.shard_map(shards, mesh=mesh, in_specs=in_specs, out_specs=out_specs, check_vma=False)
```

profile of v0, /device:TPU:25, one launch (start us, length us, event | category | flops | bytes accessed | tf_op | source)
XLA Modules:
  0.0 351.7 jit_solution(3859230590316418505)
XLA Ops:
  6.9 5.0 %all-to-all-start.1 = ((bf16[256,4,768]{2,0,1:T(8,128)(2,1)}), bf16[256,4,768]{2,0,1:T(8,128)(2,1)S(1)}, u32[]{:S(2)}, u32[]{:S(2)}) async-start(bf16[256,4,768]{2,0,1:T(8,128)(2,1)} %bitcast.77), calls=%async_computation.1 | async-start | bytes 3145728 | tf_op jit(solution)/shard_map/all_to_all | solution.py:37
  13.4 18.3 %all-to-all-done.1 = bf16[256,4,768]{2,0,1:T(8,128)(2,1)S(1)} async-done(((bf16[256,4,768]{2,0,1:T(8,128)(2,1)}), bf16[256,4,768]{2,0,1:T(8,128)(2,1)S(1)}, u32[]{:S(2)}, u32[]{:S(2)}) %all-to-all-start.1) | async-done | bytes 1572896 | tf_op jit(solution)/shard_map/all_to_all | solution.py:37
  31.7 21.3 %all_to_all.67 = bf16[256,4,768]{2,0,1:T(8,128)(2,1)S(1)} all-to-all(bf16[256,4,768]{2,0,1:T(8,128)(2,1)S(1)} %bitcast.100), channel_id=1, replica_groups=mesh['slot'=32,'ulysses'=4] {'ulysses'}, dimensions={1} | all-to-all | bytes 3145728 | tf_op jit(solution)/shard_map/all_to_all | solution.py:38
  54.1 5.4 %collective-permute-start = (bf16[2,1024,768]{2,1,0:T(8,128)(2,1)S(1)}, bf16[2,1024,768]{2,1,0:T(8,128)(2,1)S(1)}, u32[]{:S(2)}, u32[]{:S(2)}) collective-permute-start(bf16[2,1024,768]{2,1,0:T(8,128)(2,1)S(1)} %pad_maximum_fusion), channel_id=1, source_target_pairs={{0,4},{4,8},{8,12},{12,16},{16,20},{20,24},{24,28},{28,32},{32,36}... | collective-permute-start | bytes 9437192 | tf_op jit(solution)/shard_map/ppermute | solution.py:15
  59.6 34.2 %collective-permute-done = bf16[2,1024,768]{2,1,0:T(8,128)(2,1)S(1)} collective-permute-done((bf16[2,1024,768]{2,1,0:T(8,128)(2,1)S(1)}, bf16[2,1024,768]{2,1,0:T(8,128)(2,1)S(1)}, u32[]{:S(2)}, u32[]{:S(2)}) %collective-permute-start) | collective-permute-done | bytes 3145760 | tf_op jit(solution)/shard_map/ppermute | solution.py:15
  93.8 6.5 %collective-permute-start.1 = (bf16[2,1024,768]{2,1,0:T(8,128)(2,1)S(1)}, bf16[2,1024,768]{2,1,0:T(8,128)(2,1)}, u32[]{:S(2)}, u32[]{:S(2)}) collective-permute-start(bf16[2,1024,768]{2,1,0:T(8,128)(2,1)S(1)} %collective-permute-done), channel_id=1, source_target_pairs={{0,4},{4,8},{8,12},{12,16},{16,20},{20,24},{24,28},{28,32},{32,36}... | collective-permute-start | bytes 9437192 | tf_op jit(solution)/shard_map/ppermute | solution.py:15
  100.3 34.2 %collective-permute-done.1 = bf16[2,1024,768]{2,1,0:T(8,128)(2,1)} collective-permute-done((bf16[2,1024,768]{2,1,0:T(8,128)(2,1)S(1)}, bf16[2,1024,768]{2,1,0:T(8,128)(2,1)}, u32[]{:S(2)}, u32[]{:S(2)}) %collective-permute-start.1) | collective-permute-done | bytes 3145760 | tf_op jit(solution)/shard_map/ppermute | solution.py:15
  134.5 6.6 %collective-permute-start.2 = (bf16[2,1024,768]{2,1,0:T(8,128)(2,1)}, bf16[2,1024,768]{2,1,0:T(8,128)(2,1)}, u32[]{:S(2)}, u32[]{:S(2)}) collective-permute-start(bf16[2,1024,768]{2,1,0:T(8,128)(2,1)} %collective-permute-done.1), channel_id=1, source_target_pairs={{0,4},{4,8},{8,12},{12,16},{16,20},{20,24},{24,28},{28,32},{32,36}... | collective-permute-start | bytes 9437192 | tf_op jit(solution)/shard_map/ppermute | solution.py:15
  141.4 2.3 copy.50
  143.7 2.8 reduce_sum.131
  150.4 4.5 %all-to-all-start = ((bf16[256,4,768]{2,0,1:T(8,128)(2,1)}), bf16[256,4,768]{2,0,1:T(8,128)(2,1)}, u32[]{:S(2)}, u32[]{:S(2)}) async-start(bf16[256,4,768]{2,0,1:T(8,128)(2,1)} %bitcast.99), calls=%async_computation | async-start | bytes 3145728 | tf_op jit(solution)/shard_map/all_to_all | solution.py:36
  159.1 13.0 %all-to-all-done = bf16[256,4,768]{2,0,1:T(8,128)(2,1)} async-done(((bf16[256,4,768]{2,0,1:T(8,128)(2,1)}), bf16[256,4,768]{2,0,1:T(8,128)(2,1)}, u32[]{:S(2)}, u32[]{:S(2)}) %all-to-all-start) | async-done | bytes 1572896 | tf_op jit(solution)/shard_map/all_to_all | solution.py:36
  172.1 3.5 collective-permute-done.2
  175.6 146.4 %while.11 = (s32[]{:T(128)}, bf16[6,1024,128]{2,1,0:T(8,128)(2,1)}, s32[6]{0:T(128)S(1)}, bf16[1024,768]{1,0:T(8,128)(2,1)}, bf16[1024,768]{1,0:T(8,128)(2,1)}, ...) while((s32[]{:T(128)}, bf16[6,1024,128]{2,1,0:T(8,128)(2,1)}, ...), condition=%wide.region_15.16_spmd.clone, body=%wide.region_10.15_spmd.clone.sunk | while | flops 2173180928 | bytes 59302180 | solution.py:83
  180.0 2.0 fusion.140
  182.0 2.1 fusion.141
  186.1 2.2 fusion.143
  189.5 3.2 fusion.145
  197.9 2.1 fusion.149
  206.4 2.1 fusion.141
  208.5 2.0 fusion.142
  210.5 2.2 fusion.143
  213.9 3.2 fusion.145
  222.3 2.1 fusion.149
  230.8 2.1 fusion.141
  232.9 2.0 fusion.142
  234.9 2.2 fusion.143
  238.3 3.2 fusion.145
  246.7 2.1 fusion.149
  253.2 2.0 fusion.140
  255.2 2.1 fusion.141
  257.3 2.0 fusion.142
  259.3 2.2 fusion.143
  262.7 3.2 fusion.145
  271.1 2.1 fusion.149
  277.6 2.0 fusion.140
  279.6 2.1 fusion.141
  281.7 2.0 fusion.142
  283.7 2.2 fusion.143
  287.1 3.2 fusion.145
  295.5 2.1 fusion.149
  304.0 2.1 fusion.141
  306.1 2.0 fusion.142
  308.1 2.2 fusion.143
  311.5 3.2 fusion.145
  319.9 2.1 fusion.149
  327.0 3.6 %all-to-all-start.3 = ((bf16[4,256,768]{1,2,0:T(8,128)(2,1)}), bf16[4,256,768]{1,2,0:T(8,128)(2,1)S(1)}, u32[]{:S(2)}, u32[]{:S(2)}) async-start(bf16[4,256,768]{1,2,0:T(8,128)(2,1)} %copy.45), calls=%async_computation.3 | async-start | bytes 3145728 | tf_op jit(solution)/shard_map/all_to_all | solution.py:87
  332.1 17.4 %all-to-all-done.3 = bf16[4,256,768]{1,2,0:T(8,128)(2,1)S(1)} async-done(((bf16[4,256,768]{1,2,0:T(8,128)(2,1)}), bf16[4,256,768]{1,2,0:T(8,128)(2,1)S(1)}, u32[]{:S(2)}, u32[]{:S(2)}) %all-to-all-start.3) | async-done | bytes 1572896 | tf_op jit(solution)/shard_map/all_to_all | solution.py:87
  (109 shorter events, 92.4 us)
Async XLA Ops:
  0.0 3.5 copy-start
  3.3 1.4 copy-start.4
  6.9 24.8 %all-to-all-start.1 = ((bf16[256,4,768]{2,0,1:T(8,128)(2,1)}), bf16[256,4,768]{2,0,1:T(8,128)(2,1)S(1)}, u32[]{:S(2)}, u32[]{:S(2)}) async-start(bf16[256,4,768]{2,0,1:T(8,128)(2,1)} %bitcast.77), calls=%async_computation.1 | async-start | bytes 3145728 | tf_op jit(solution)/shard_map/all_to_all | solution.py:37
  31.7 21.3 %copy-start.2 = (bf16[256,4,768]{2,0,1:T(8,128)(2,1)}, bf16[256,4,768]{2,0,1:T(8,128)(2,1)S(1)}, u32[]{:S(2)}) copy-start(bf16[256,4,768]{2,0,1:T(8,128)(2,1)S(1)} %all-to-all-done.1) | copy-start | bytes 4718596
  53.0 1.1 copy-start.3
  53.0 88.1 %copy-start.5 = (bf16[256,3072]{1,0:T(8,128)(2,1)S(1)}, bf16[256,3072]{1,0:T(8,128)(2,1)}, u32[]{:S(2)}) copy-start(bf16[256,3072]{1,0:T(8,128)(2,1)} %param.11) | copy-start | bytes 4718596
  54.1 39.6 %collective-permute-start = (bf16[2,1024,768]{2,1,0:T(8,128)(2,1)S(1)}, bf16[2,1024,768]{2,1,0:T(8,128)(2,1)S(1)}, u32[]{:S(2)}, u32[]{:S(2)}) collective-permute-start(bf16[2,1024,768]{2,1,0:T(8,128)(2,1)S(1)} %pad_maximum_fusion), channel_id=1, source_target_pairs={{0,4},{4,8},{8,12},{12,16},{16,20},{20,24},{24,28},{28,32},{32,36}... | collective-permute-start | bytes 9437192 | tf_op jit(solution)/shard_map/ppermute | solution.py:15
  93.8 40.7 %collective-permute-start.1 = (bf16[2,1024,768]{2,1,0:T(8,128)(2,1)S(1)}, bf16[2,1024,768]{2,1,0:T(8,128)(2,1)}, u32[]{:S(2)}, u32[]{:S(2)}) collective-permute-start(bf16[2,1024,768]{2,1,0:T(8,128)(2,1)S(1)} %collective-permute-done), channel_id=1, source_target_pairs={{0,4},{4,8},{8,12},{12,16},{16,20},{20,24},{24,28},{28,32},{32,36}... | collective-permute-start | bytes 9437192 | tf_op jit(solution)/shard_map/ppermute | solution.py:15
  134.5 41.1 %collective-permute-start.2 = (bf16[2,1024,768]{2,1,0:T(8,128)(2,1)}, bf16[2,1024,768]{2,1,0:T(8,128)(2,1)}, u32[]{:S(2)}, u32[]{:S(2)}) collective-permute-start(bf16[2,1024,768]{2,1,0:T(8,128)(2,1)} %collective-permute-done.1), channel_id=1, source_target_pairs={{0,4},{4,8},{8,12},{12,16},{16,20},{20,24},{24,28},{28,32},{32,36}... | collective-permute-start | bytes 9437192 | tf_op jit(solution)/shard_map/ppermute | solution.py:15
  143.7 3.0 copy-start.8
  146.7 1.4 copy-start.6
  149.1 5.9 %copy-start.9 = (s32[32]{0:T(128)S(1)}, s32[32]{0:T(128)}, u32[]{:S(2)}) copy-start(s32[32]{0:T(128)} %param.18) | copy-start | bytes 388
  149.1 5.9 %copy-start.10 = (s32[32]{0:T(128)S(1)}, s32[32]{0:T(128)}, u32[]{:S(2)}) copy-start(s32[32]{0:T(128)} %param.19) | copy-start | bytes 388
  150.4 21.7 %all-to-all-start = ((bf16[256,4,768]{2,0,1:T(8,128)(2,1)}), bf16[256,4,768]{2,0,1:T(8,128)(2,1)}, u32[]{:S(2)}, u32[]{:S(2)}) async-start(bf16[256,4,768]{2,0,1:T(8,128)(2,1)} %bitcast.99), calls=%async_computation | async-start | bytes 3145728 | tf_op jit(solution)/shard_map/all_to_all | solution.py:36
  325.6 4.9 %copy-start.11 = (s32[32]{0:T(128)S(1)}, s32[32]{0:T(128)}, u32[]{:S(2)}) copy-start(s32[32]{0:T(128)} %param.17) | copy-start | bytes 388
  325.6 6.4 %copy-start.7 = (f32[16,3072]{1,0:T(8,128)S(1)}, f32[16,3072]{1,0:T(8,128)}, u32[]{:S(2)}) copy-start(f32[16,3072]{1,0:T(8,128)} %param.16) | copy-start | bytes 589828
  327.0 22.5 %all-to-all-start.3 = ((bf16[4,256,768]{1,2,0:T(8,128)(2,1)}), bf16[4,256,768]{1,2,0:T(8,128)(2,1)S(1)}, u32[]{:S(2)}, u32[]{:S(2)}) async-start(bf16[4,256,768]{1,2,0:T(8,128)(2,1)} %copy.45), calls=%async_computation.3 | async-start | bytes 3145728 | tf_op jit(solution)/shard_map/all_to_all | solution.py:87
  332.0 19.7 %copy-start.1 = (f32[128]{0:T(128)S(1)}, f32[128]{0:T(128)}, u32[]{:S(2)}) copy-start(f32[128]{0:T(128)} %param.15) | copy-start | bytes 1540
where the time goes:
time: 354 us; the launch traced here: 352 us
  waiting for transfers between devices  121 us (34%)
  matrix products  92.8 us (26%)
  local copies, waits for them, and re-layouts  51.3 us (14%)
  starting transfers between devices  31.7 us (9%)
  other arithmetic  26.8 us (8%)
  blocking collectives  21.3 us (6%)
  loops' own time  4.26 us (1%)
    ppermute x3, waiting for transfers between devices, from_behind(): return lax.ppermute(block, axis, route)  71.9 us
    dot_general x24, matrix products, one_head(): lax.dot_general(query_block, key_block, (((1,), (1,)), ((), ())), preferr...  47.3 us
    dot_general x24, matrix products, one_head(): jnp.dot(weight.astype(jnp.bfloat16), value_block, preferred_element_type=...  45.5 us
    slice x12, local copies, waits for them, and re-layouts, one_head(): value_block = lax.dynamic_slice_in_dim(blocks[offset][1], start, HD, 1)  30.7 us
    all_to_all x1, blocking collectives, shards(): lax.all_to_all(value_states, 'ulysses', split_axis=1, concat_axis=0, tile...  21.3 us
    ppermute x3, starting transfers between devices, from_behind(): return lax.ppermute(block, axis, route)  18.5 us
    all_to_all x1, waiting for transfers between devices, shards(): lax.all_to_all(k_norm, 'ulysses', split_axis=1, concat_axis=0, tiled=True)  18.3 us
    all_to_all x1, waiting for transfers between devices, shards(): lax.all_to_all(attended, 'ulysses', split_axis=0, concat_axis=1, tiled=True)  17.4 us
  transfers between devices with their start and end apart: 6, of which 6 were waited for; matrix products, arithmetic and copies ran while one was open for 4% of the time, Pallas kernels for 0%

commit v1 on v0

v1 whole, which is shorter than its diff:
```python
import functools
import math

import jax
import jax.numpy as jnp
from jax import lax
from jax.experimental import pallas as pl
from jax.experimental.pallas import tpu as pltpu
from jax.sharding import PartitionSpec as P

HD = 128
CORES = 2
MESH = pl.DeviceIdType.MESH
FACTOR = math.log2(math.e) / math.sqrt(HD)
F32, BF16 = jnp.float32, jnp.bfloat16


def kernel(
    slots, depth, lengths, context, query_gain, key_gain, q_hbm, k_hbm, v_hbm, out_hbm,
    q_in, k_in, v_in, q_own, k_own, v_own, q_far, local, ahead, part, part_sum, back, back_sum, done,
    load_sem, in_send, in_recv, q_send, q_recv, part_send, part_recv, out_send, out_recv,
):
    slot, z = lax.axis_index("slot"), lax.axis_index("ulysses")
    chip, core = slot // CORES, slot % CORES
    chips = slots // CORES
    heads = q_own.shape[0]
    span = q_own.shape[2]
    rows = span // depth
    mine = z * CORES + core
    partners = depth * CORES
    tile = min(256, span)
    blocks = span // HD

    def chip_at(distance):
        return ((chip + distance + chips) % chips) * CORES + core, z

    def partner(r):
        return chip * CORES + (core + r % CORES) % CORES, (z + r // CORES) % depth

    loads = [
        pltpu.make_async_copy(source, target, load_sem.at[i])
        for i, (source, target) in enumerate(((q_hbm, q_in), (k_hbm, k_in), (v_hbm, v_in)))
    ]
    for load in loads:
        load.start()

    barrier = pltpu.get_barrier_semaphore()
    everyone = [partner(r) for r in range(1, partners)] + [chip_at(d) for d in (-2, -1, 1, 2)]
    for other in everyone:
        pl.semaphore_signal(barrier, inc=1, device_id=other, device_id_type=MESH)

    def group(distance):
        return (chip * CORES + distance) % slots

    for g in range(CORES):
        used = lax.broadcasted_iota(jnp.int32, (span, HD), 0) < lengths[group(g)]
        ones = jnp.where(used, 1.0, 0.0).astype(BF16)
        for j in range(heads):
            v_own[j, g, :, HD:] = ones

    for load in loads:
        load.wait()
    pl.semaphore_wait(barrier, len(everyone))

    def columns(owner, j):
        return pl.ds(pl.multiple_of((owner * heads + j) * HD, HD), HD)

    own_rows = pl.ds(pl.multiple_of(z * rows, rows), rows)

    def normalize(ref, cols, gain):
        full = ref[:, cols].astype(F32)
        square = jnp.mean(full * full, axis=-1, keepdims=True)
        ref[:, cols] = (full * lax.rsqrt(square + 1e-06) * gain[...]).astype(BF16)

    def clip_values(cols):
        place = lax.broadcasted_iota(jnp.int32, (rows, HD), 0) + z * rows
        v_in[:, cols] = jnp.where(place < lengths[slot], v_in[:, cols].astype(F32), 0.0).astype(BF16)

    def landing(which, j):
        if which == 2:
            return v_own.at[j, :, :, pl.ds(0, HD)]
        return (q_own, k_own)[which].at[j]

    def send_in(which, j):
        source = (q_in, k_in, v_in)[which]
        if which == 2:
            target = v_own.at[j, core, own_rows, pl.ds(0, HD)]
        else:
            target = (q_own, k_own)[which].at[j, core, own_rows, :]

        def one(r, carry):
            to_slot, to_z = partner(r)
            cols = columns(to_z * CORES + to_slot % CORES, j)
            if which == 0:
                normalize(source, cols, query_gain)
            elif which == 1:
                normalize(source, cols, key_gain)
            else:
                clip_values(cols)

            @pl.when(r == 0)
            def _():
                pltpu.make_async_copy(source.at[:, cols], target, in_recv.at[which, j]).start()

            @pl.when(r > 0)
            def _():
                pltpu.make_async_remote_copy(
                    src_ref=source.at[:, cols], dst_ref=target,
                    send_sem=in_send.at[which, j], recv_sem=in_recv.at[which, j],
                    device_id=(to_slot, to_z), device_id_type=MESH,
                ).start()

            return carry

        lax.fori_loop(0, partners, one, 0)

    def await_in(which, j):
        here = landing(which, j)
        pltpu.make_async_copy(here, here, in_recv.at[which, j]).wait()

    def query_copy(j, n):
        return pltpu.make_async_remote_copy(
            src_ref=q_own.at[j, n % 2], dst_ref=q_far.at[j, n],
            send_sem=q_send.at[j, n], recv_sem=q_recv.at[j, n],
            device_id=chip_at(-2 if n == 2 else -1), device_id_type=MESH,
        )

    def part_copies(j, n):
        return [
            pltpu.make_async_remote_copy(
                src_ref=source.at[j, n], dst_ref=target.at[j, n],
                send_sem=part_send.at[j, n, i], recv_sem=part_recv.at[j, n, i],
                device_id=chip_at(1), device_id_type=MESH,
            )
            for i, (source, target) in enumerate(((part, back), (part_sum, back_sum)))
        ]

    def attend(queries, j, g):
        scores = lax.dot_general(
            queries, k_own[j, g], (((1,), (1,)), ((), ())), preferred_element_type=F32
        )
        weight = jnp.exp2(scores * FACTOR).astype(BF16)
        return jnp.dot(weight, v_own[j, g], preferred_element_type=F32)

    def allowed(distance, offset):
        return jnp.where(context[group(distance)] >= offset, 1.0, 0.0)

    def tiles(body):
        def one(i, carry):
            body(i, pl.ds(pl.multiple_of(i * tile, tile), tile))
            return carry

        lax.fori_loop(0, span // tile, one, 0)

    diagonal = lax.broadcasted_iota(jnp.int32, (HD, HD), 0) == lax.broadcasted_iota(jnp.int32, (HD, HD), 1)

    def keep_part(j, n, i, here, both, arrived):
        number = both[:, :HD]
        if arrived is not None:
            number = number + back[j, arrived, here, :].astype(F32)
        part[j, n, here, :] = number.astype(BF16)
        for s in range(tile // HD):
            line = pl.ds(i * (tile // HD) + s, 1)
            total = both[s * HD:(s + 1) * HD, HD:]
            total = jnp.sum(jnp.where(diagonal, total, 0.0), axis=0, keepdims=True)
            if arrived is not None:
                total = total + back_sum[j, arrived, line, :]
            part_sum[j, n, line, :] = total

    def send_parts(j, n):
        for copy in part_copies(j, n):
            copy.start()

    def queries_out(j):
        await_in(0, j)
        for n in (2, 0, 1):
            query_copy(j, n).start()

    def own_part(j):
        def body(i, here):
            local[j, 0, here, :] = attend(q_own[j, 0, here, :], j, 0)
            queries = q_own[j, 1, here, :]
            local[j, 1, here, :] = attend(queries, j, 1) + allowed(1, 1) * attend(queries, j, 0)

        tiles(body)

    def part_c(j):
        query_copy(j, 2).wait_recv()

        def body(i, here):
            both = allowed(4, 3) * attend(q_far[j, 2, here, :], j, 1)
            keep_part(j, 2, i, here, both, None)

        tiles(body)
        send_parts(j, 2)

    def part_b(j):
        query_copy(j, 1).wait_recv()

        def body(i, here):
            queries = q_far[j, 1, here, :]
            both = allowed(3, 2) * attend(queries, j, 1) + allowed(3, 3) * attend(queries, j, 0)
            keep_part(j, 1, i, here, both, None)

        tiles(body)
        send_parts(j, 1)

    def part_a_begin(j):
        query_copy(j, 0).wait_recv()

        def body(i, here):
            queries = q_far[j, 0, here, :]
            ahead[here, :] = allowed(2, 1) * attend(queries, j, 1) + allowed(2, 2) * attend(queries, j, 0)

        tiles(body)

    def part_a_end(j):
        for copy in part_copies(j, 2):
            copy.wait_recv()
        tiles(lambda i, here: keep_part(j, 0, i, here, ahead[here, :], 2))
        send_parts(j, 0)

    def finish(j, g):
        for copy in part_copies(j, g):
            copy.wait_recv()
        used = lengths[group(g)]

        def body(i, carry):
            here = pl.ds(pl.multiple_of(i * HD, HD), HD)
            both = local[j, g, here, :]
            number = both[:, :HD] + back[j, g, here, :].astype(F32)
            line = back_sum[j, g, pl.ds(i, 1), :]
            total = both[:, HD:] + jnp.broadcast_to(line, (HD, HD)).T
            place = lax.broadcasted_iota(jnp.int32, (HD, HD), 0) + i * HD
            done[j, g, here, :] = jnp.where(place < used, number / total, 0.0).astype(BF16)
            return carry

        lax.fori_loop(0, blocks, body, 0)
        target = out_hbm.at[:, columns(mine, j)]
        for d in range(depth):
            to_z = (z + d) % depth
            source = done.at[j, g, pl.ds(pl.multiple_of(to_z * rows, rows), rows), :]
            to_slot = chip * CORES + g

            @pl.when((to_slot == slot) & (to_z == z))
            def _():
                pltpu.make_async_copy(source, target, out_recv.at[j]).start()

            @pl.when((to_slot != slot) | (to_z != z))
            def _():
                pltpu.make_async_remote_copy(
                    src_ref=source, dst_ref=target, send_sem=out_send.at[j], recv_sem=out_recv.at[j],
                    device_id=(to_slot, to_z), device_id_type=MESH,
                ).start()

    def keys_in(j):
        await_in(1, j)
        await_in(2, j)

    for j in range(heads):
        for which in range(3):
            send_in(which, j)
    queries_out(0)
    keys_in(0)
    own_part(0)
    part_c(0)
    part_b(0)
    part_a_begin(0)
    for j in range(1, heads):
        queries_out(j)
        part_a_end(j - 1)
        keys_in(j)
        own_part(j)
        part_c(j)
        part_b(j)
        part_a_begin(j)
        finish(j - 1, 1)
        finish(j - 1, 0)
    part_a_end(heads - 1)
    finish(heads - 1, 1)
    finish(heads - 1, 0)

    sent = q_in.at[:, pl.ds(0, (partners - 1) * HD)]
    got = q_in.at[:, pl.ds(0, partners * HD)]
    for j in range(heads):
        pltpu.make_async_copy(got, got, out_recv.at[j]).wait()
        pltpu.make_async_copy(sent, sent, out_send.at[j]).wait()
        for which in range(3):
            pltpu.make_async_copy(sent, sent, in_send.at[which, j]).wait()
        for n in range(3):
            query_copy(j, n).wait_send()
            for copy in part_copies(j, n):
                copy.wait_send()


def attention(slots, depth, lengths, context, query_gain, key_gain, queries, key_states, value_states):
    rows, width = queries.shape
    heads = width // (HD * depth * CORES)
    span = rows * depth
    row = pltpu.VMEM((rows, width), BF16)
    lines = (heads, 3, span // HD, HD)
    dma = pltpu.SemaphoreType.DMA
    return pl.pallas_call(
        functools.partial(kernel, slots, depth),
        out_shape=jax.ShapeDtypeStruct((rows, width), BF16),
        in_specs=[pl.BlockSpec(memory_space=pltpu.SMEM)] * 2
        + [pl.BlockSpec(memory_space=pltpu.VMEM)] * 2
        + [pl.BlockSpec(memory_space=pl.ANY)] * 3,
        out_specs=pl.BlockSpec(memory_space=pl.ANY),
        scratch_shapes=[
            row, row, row,
            pltpu.VMEM((heads, CORES, span, HD), BF16),
            pltpu.VMEM((heads, CORES, span, HD), BF16),
            pltpu.VMEM((heads, CORES, span, 2 * HD), BF16),
            pltpu.VMEM((heads, 3, span, HD), BF16),
            pltpu.VMEM((heads, CORES, span, 2 * HD), F32),
            pltpu.VMEM((span, 2 * HD), F32),
            pltpu.VMEM((heads, 3, span, HD), BF16),
            pltpu.VMEM(lines, F32),
            pltpu.VMEM((heads, 3, span, HD), BF16),
            pltpu.VMEM(lines, F32),
            pltpu.VMEM((heads, CORES, span, HD), BF16),
            dma((3,)), dma((3, heads)), dma((3, heads)), dma((heads, 3)), dma((heads, 3)),
            dma((heads, 3, 2)), dma((heads, 3, 2)), dma((heads,)), dma((heads,)),
        ],
        compiler_params=pltpu.CompilerParams(
            collective_id=0, has_side_effects=True, vmem_limit_bytes=50 * 2**20
        ),
        cost_estimate=pl.CostEstimate(
            flops=32 * heads * span * span * HD, bytes_accessed=8 * rows * width,
            transcendentals=8 * heads * span * span,
        ),
    )(lengths, context, query_gain[None, :], key_gain[None, :], queries, key_states, value_states)


def shards(
    slots, depth, queries, key_states, value_states, query_gain, key_gain, level_gate, levels, lengths, context
):
    attended = attention(
        slots, depth, lengths, context, query_gain, key_gain, queries, key_states, value_states
    )
    level_here = levels[lax.axis_index("slot")]
    gate_row = lax.dynamic_slice_in_dim(level_gate, level_here, 1, 0)
    return (gate_row * attended.astype(F32)).astype(BF16)


def solution(mesh):
    split = P(("slot", "ulysses"), None)
    return jax.shard_map(
        functools.partial(shards, mesh.shape["slot"], mesh.shape["ulysses"]),
        mesh=mesh,
        in_specs=(split, split, split) + (P(),) * 6,
        out_specs=split,
        check_vma=False,
    )
```

time: 354 us -> 126 us (0.36)
  the two profiles are of different devices: /device:TPU:25 before, /device:TPU:0 now
where the time goes in v1:
time: 126 us
  Pallas kernels  117 us (93%)
  local copies, waits for them, and re-layouts  5.32 us (4%)
  between operations  1.98 us (2%)
  other arithmetic  1.47 us (1%)
    pallas_call x1, Pallas kernels, attention(): pl.pallas_call(functools.partial(kernel, slots, depth), out_shape=jax.Sha...  117 us
    unnamed x12, local copies, waits for them, and re-layouts  4.03 us

profile of v1, /device:TPU:0, one launch (start us, length us, event | category | flops | bytes accessed | tf_op | source)
XLA Modules:
  0.0 125.7 jit_solution(9918917835497365741)
XLA Ops:
  0.0 0.0 copy-start
  0.0 1.3 %dynamic_slice.6 = s32[1]{0:T(128)} dynamic-slice(s32[32]{0:T(128)} %param.15, s32[]{:T(128)S(6)} %select_n.6), dynamic_slice_sizes={1} | dynamic-slice | bytes 12 | tf_op jit(solution)/shard_map/dynamic_slice | solution.py:342
  3.2 0.0 copy-done
  3.3 0.0 copy-start.1
  3.3 1.4 %copy-done.1 = bf16[256,3072]{1,0:T(8,128)(2,1)S(1)} copy-done((bf16[256,3072]{1,0:T(8,128)(2,1)S(1)}, bf16[256,3072]{1,0:T(8,128)(2,1)}, u32[]{:S(2)}) %copy-start.1) | copy-done | bytes 1572888
  4.7 0.0 copy-start.2
  4.7 0.7 copy-done.2
  5.3 0.0 copy-start.3
  5.3 0.7 copy-done.3
  6.0 0.0 copy-start.4
  6.0 0.7 copy-done.4
  6.6 0.0 copy-start.5
  6.6 0.7 copy-done.5
  7.3 116.9 %shard_map.91 = bf16[256,3072]{1,0:T(8,128)(2,1)S(1)} custom-call(s32[32]{0:T(128)S(1)} %copy-done.2, s32[32]{0:T(128)S(1)} %copy-done.3, f32[1,128]{1,0:T(1,128)S(1)} %bitcast.4, f32[1,128]{1,0:T(1,128)S(1)} %bitcast.5, bf16[256,3072]{1,0:T(8,128)(2,1)S(1)} %copy-done.1, bf16[256,3072]{1,0:T(8,128)(2,1)} %k_hbm.1, bf16[256,3072]{1,0:T(8,128)(2,1)} %v_hbm.1), custom_call_target="tpu_custom_call" | custom-call | flops 12884901888 | bytes 6291456 | tf_op jit(solution)/shard_map/pallas_call | solution.py:303
  124.2 1.5 %multiply_convert_fusion = bf16[256,3072]{1,0:T(8,128)(2,1)} fusion(bf16[256,3072]{1,0:T(8,128)(2,1)S(1)} %shard_map.91, f32[3072]{0:T(1024)S(1)} %bitcast.6), kind=kLoop, calls=%fused_computation | loop fusion | flops 2359296 | bytes 3158016 | tf_op jit(solution)/shard_map/convert_element_type | solution.py:344
  (1 shorter events, 0.0 us)
Async XLA Ops:
  0.0 3.2 %copy-start = (f32[16,3072]{1,0:T(8,128)S(1)}, f32[16,3072]{1,0:T(8,128)}, u32[]{:S(2)}) copy-start(f32[16,3072]{1,0:T(8,128)} %param.14) | copy-start | bytes 589828
  3.3 1.4 %copy-start.1 = (bf16[256,3072]{1,0:T(8,128)(2,1)S(1)}, bf16[256,3072]{1,0:T(8,128)(2,1)}, u32[]{:S(2)}) copy-start(bf16[256,3072]{1,0:T(8,128)(2,1)} %q_hbm.1) | copy-start | bytes 4718596
  4.7 0.7 copy-start.2
  5.3 0.7 copy-start.3
  6.0 0.7 copy-start.4
  6.6 0.7 copy-start.5

commit v2 on v1

--- a/solution.py
+++ b/solution.py
@@ -16,8 +16,9 @@
 
 
 def kernel(
-    slots, depth, lengths, context, query_gain, key_gain, q_hbm, k_hbm, v_hbm, out_hbm,
-    q_in, k_in, v_in, q_own, k_own, v_own, q_far, local, ahead, part, part_sum, back, back_sum, done,
+    slots, depth, levels_hbm, lengths_hbm, context_hbm, query_gain_hbm, key_gain_hbm, gate_hbm,
+    q_hbm, k_hbm, v_hbm, out_hbm,
+    levels, lengths, context, query_gain, key_gain, gate, q_in, k_in, v_in, q_own, k_own, v_own, q_far, local, ahead, part, part_sum, back, back_sum, done,
     load_sem, in_send, in_recv, q_send, q_recv, part_send, part_recv, out_send, out_recv,
 ):
     slot, z = lax.axis_index("slot"), lax.axis_index("ulysses")
@@ -28,7 +29,7 @@
     rows = span // depth
     mine = z * CORES + core
     partners = depth * CORES
-    tile = min(256, span)
+    tile = span
     blocks = span // HD
 
     def chip_at(distance):
@@ -39,7 +40,11 @@
 
     loads = [
         pltpu.make_async_copy(source, target, load_sem.at[i])
-        for i, (source, target) in enumerate(((q_hbm, q_in), (k_hbm, k_in), (v_hbm, v_in)))
+        for i, (source, target) in enumerate((
+            (lengths_hbm, lengths), (query_gain_hbm, query_gain), (key_gain_hbm, key_gain),
+            (q_hbm, q_in), (k_hbm, k_in), (v_hbm, v_in),
+            (context_hbm, context), (levels_hbm, levels), (gate_hbm, gate),
+        ))
     ]
     for load in loads:
         load.start()
@@ -52,13 +57,14 @@
     def group(distance):
         return (chip * CORES + distance) % slots
 
+    loads[0].wait()
     for g in range(CORES):
         used = lax.broadcasted_iota(jnp.int32, (span, HD), 0) < lengths[group(g)]
         ones = jnp.where(used, 1.0, 0.0).astype(BF16)
         for j in range(heads):
             v_own[j, g, :, HD:] = ones
 
-    for load in loads:
+    for load in loads[1:]:
         load.wait()
     pl.semaphore_wait(barrier, len(everyone))
 
@@ -76,10 +82,10 @@
         place = lax.broadcasted_iota(jnp.int32, (rows, HD), 0) + z * rows
         v_in[:, cols] = jnp.where(place < lengths[slot], v_in[:, cols].astype(F32), 0.0).astype(BF16)
 
-    def landing(which, j):
+    def landing(which, j, g):
         if which == 2:
-            return v_own.at[j, :, :, pl.ds(0, HD)]
-        return (q_own, k_own)[which].at[j]
+            return v_own.at[j, g, :, pl.ds(0, HD)]
+        return (q_own, k_own)[which].at[j, g]
 
     def send_in(which, j):
         source = (q_in, k_in, v_in)[which]
@@ -100,13 +106,13 @@
 
             @pl.when(r == 0)
             def _():
-                pltpu.make_async_copy(source.at[:, cols], target, in_recv.at[which, j]).start()
+                pltpu.make_async_copy(source.at[:, cols], target, in_recv.at[which, j, core]).start()
 
             @pl.when(r > 0)
             def _():
                 pltpu.make_async_remote_copy(
                     src_ref=source.at[:, cols], dst_ref=target,
-                    send_sem=in_send.at[which, j], recv_sem=in_recv.at[which, j],
+                    send_sem=in_send.at[which, j], recv_sem=in_recv.at[which, j, core],
                     device_id=(to_slot, to_z), device_id_type=MESH,
                 ).start()
 
@@ -114,15 +120,16 @@
 
         lax.fori_loop(0, partners, one, 0)
 
-    def await_in(which, j):
-        here = landing(which, j)
-        pltpu.make_async_copy(here, here, in_recv.at[which, j]).wait()
+    def await_in(which, j, g):
+        here = landing(which, j, g)
+        pltpu.make_async_copy(here, here, in_recv.at[which, j, g]).wait()
 
     def query_copy(j, n):
+        direct = n == 2 and j == 0
         return pltpu.make_async_remote_copy(
-            src_ref=q_own.at[j, n % 2], dst_ref=q_far.at[j, n],
+            src_ref=q_far.at[j, 0] if n == 2 and not direct else q_own.at[j, n % 2], dst_ref=q_far.at[j, n],
             send_sem=q_send.at[j, n], recv_sem=q_recv.at[j, n],
-            device_id=chip_at(-2 if n == 2 else -1), device_id_type=MESH,
+            device_id=chip_at(-2 if direct else -1), device_id_type=MESH,
         )
 
     def part_copies(j, n):
@@ -171,14 +178,29 @@
         for copy in part_copies(j, n):
             copy.start()
 
-    def queries_out(j):
-        await_in(0, j)
-        for n in (2, 0, 1):
-            query_copy(j, n).start()
-
-    def own_part(j):
+    def query_a_out(j):
+        await_in(0, j, 0)
+        if j == 0:
+            query_copy(j, 2).start()
+        query_copy(j, 0).start()
+
+    def query_b_out(j):
+        await_in(0, j, 1)
+        query_copy(j, 1).start()
+
+    def query_on(j):
+        query_copy(j, 0).wait_recv()
+        if j > 0:
+            query_copy(j, 2).start()
+
+    def own_a(j):
         def body(i, here):
             local[j, 0, here, :] = attend(q_own[j, 0, here, :], j, 0)
+
+        tiles(body)
+
+    def own_b(j):
+        def body(i, here):
             queries = q_own[j, 1, here, :]
             local[j, 1, here, :] = attend(queries, j, 1) + allowed(1, 1) * attend(queries, j, 0)
 
@@ -206,8 +228,6 @@
         send_parts(j, 1)
 
     def part_a_begin(j):
-        query_copy(j, 0).wait_recv()
-
         def body(i, here):
             queries = q_far[j, 0, here, :]
             ahead[here, :] = allowed(2, 1) * attend(queries, j, 1) + allowed(2, 2) * attend(queries, j, 0)
@@ -224,6 +244,8 @@
         for copy in part_copies(j, g):
             copy.wait_recv()
         used = lengths[group(g)]
+        levels_here = lax.broadcasted_iota(jnp.int32, (gate.shape[0], HD), 0) == levels[group(g)]
+        gate_row = jnp.sum(jnp.where(levels_here, gate[:, columns(mine, j)], 0.0), axis=0, keepdims=True)
 
         def body(i, carry):
             here = pl.ds(pl.multiple_of(i * HD, HD), HD)
@@ -232,7 +254,8 @@
             line = back_sum[j, g, pl.ds(i, 1), :]
             total = both[:, HD:] + jnp.broadcast_to(line, (HD, HD)).T
             place = lax.broadcasted_iota(jnp.int32, (HD, HD), 0) + i * HD
-            done[j, g, here, :] = jnp.where(place < used, number / total, 0.0).astype(BF16)
+            attended = jnp.where(place < used, number / total, 0.0).astype(BF16)
+            done[j, g, here, :] = (gate_row * attended.astype(F32)).astype(BF16)
             return carry
 
         lax.fori_loop(0, blocks, body, 0)
@@ -253,32 +276,51 @@
                     device_id=(to_slot, to_z), device_id_type=MESH,
                 ).start()
 
-    def keys_in(j):
-        await_in(1, j)
-        await_in(2, j)
-
+    def keys_in(j, g):
+        await_in(1, j, g)
+        await_in(2, j, g)
+
+    def heads_in(j):
+        @pl.when(core == 0)
+        def _():
+            for which in (0, 1, 2):
+                send_in(which, j)
+
+        @pl.when(core != 0)
+        def _():
+            for which in (1, 2, 0):
+                send_in(which, j)
+
+    last = heads - 1
     for j in range(heads):
-        for which in range(3):
-            send_in(which, j)
-    queries_out(0)
-    keys_in(0)
-    own_part(0)
-    part_c(0)
-    part_b(0)
-    part_a_begin(0)
-    for j in range(1, heads):
-        queries_out(j)
-        part_a_end(j - 1)
-        keys_in(j)
-        own_part(j)
+        heads_in(j)
+        if j == 0:
+            query_a_out(0)
+    query_on(0)
+    for j in range(heads):
+        keys_in(j, 1)
+        if j > 0:
+            query_b_out(j)
         part_c(j)
+        if j == 0:
+            query_b_out(j)
+        keys_in(j, 0)
+        if j == last:
+            for i in range(last - 1):
+                finish(i, 0)
+                finish(i, 1)
+        part_a_begin(j)
+        own_a(j)
+        if j < last:
+            query_a_out(j + 1)
+        part_a_end(j)
         part_b(j)
-        part_a_begin(j)
-        finish(j - 1, 1)
-        finish(j - 1, 0)
-    part_a_end(heads - 1)
-    finish(heads - 1, 1)
-    finish(heads - 1, 0)
+        if j < last:
+            query_on(j + 1)
+        own_b(j)
+    for j in range(max(last - 1, 0), heads):
+        finish(j, 0)
+        finish(j, 1)
 
     sent = q_in.at[:, pl.ds(0, (partners - 1) * HD)]
     got = q_in.at[:, pl.ds(0, partners * HD)]
@@ -293,7 +335,7 @@
                 copy.wait_send()
 
 
-def attention(slots, depth, lengths, context, query_gain, key_gain, queries, key_states, value_states):
+def attention(slots, depth, levels, lengths, context, query_gain, key_gain, level_gate, queries, key_states, value_states):
     rows, width = queries.shape
     heads = width // (HD * depth * CORES)
     span = rows * depth
@@ -303,11 +345,12 @@
     return pl.pallas_call(
         functools.partial(kernel, slots, depth),
         out_shape=jax.ShapeDtypeStruct((rows, width), BF16),
-        in_specs=[pl.BlockSpec(memory_space=pltpu.SMEM)] * 2
-        + [pl.BlockSpec(memory_space=pltpu.VMEM)] * 2
-        + [pl.BlockSpec(memory_space=pl.ANY)] * 3,
+        in_specs=[pl.BlockSpec(memory_space=pl.ANY)] * 9,
         out_specs=pl.BlockSpec(memory_space=pl.ANY),
         scratch_shapes=[
+            pltpu.SMEM(levels.shape, jnp.int32), pltpu.SMEM(lengths.shape, jnp.int32),
+            pltpu.SMEM(context.shape, jnp.int32),
+            pltpu.VMEM((1, HD), F32), pltpu.VMEM((1, HD), F32), pltpu.VMEM(level_gate.shape, F32),
             row, row, row,
             pltpu.VMEM((heads, CORES, span, HD), BF16),
             pltpu.VMEM((heads, CORES, span, HD), BF16),
@@ -320,28 +363,29 @@
             pltpu.VMEM((heads, 3, span, HD), BF16),
             pltpu.VMEM(lines, F32),
             pltpu.VMEM((heads, CORES, span, HD), BF16),
-            dma((3,)), dma((3, heads)), dma((3, heads)), dma((heads, 3)), dma((heads, 3)),
+            dma((9,)), dma((3, heads)), dma((3, heads, CORES)), dma((heads, 3)), dma((heads, 3)),
             dma((heads, 3, 2)), dma((heads, 3, 2)), dma((heads,)), dma((heads,)),
         ],
         compiler_params=pltpu.CompilerParams(
-            collective_id=0, has_side_effects=True, vmem_limit_bytes=50 * 2**20
+            collective_id=0, has_side_effects=True, vmem_limit_bytes=60 * 2**20
         ),
         cost_estimate=pl.CostEstimate(
             flops=32 * heads * span * span * HD, bytes_accessed=8 * rows * width,
             transcendentals=8 * heads * span * span,
         ),
-    )(lengths, context, query_gain[None, :], key_gain[None, :], queries, key_states, value_states)
+    )(
+        levels, lengths, context, query_gain[None, :], key_gain[None, :], level_gate,
+        queries, key_states, value_states,
+    )
 
 
 def shards(
     slots, depth, queries, key_states, value_states, query_gain, key_gain, level_gate, levels, lengths, context
 ):
-    attended = attention(
-        slots, depth, lengths, context, query_gain, key_gain, queries, key_states, value_states
+    return attention(
+        slots, depth, levels, lengths, context, query_gain, key_gain, level_gate,
+        queries, key_states, value_states,
     )
-    level_here = levels[lax.axis_index("slot")]
-    gate_row = lax.dynamic_slice_in_dim(level_gate, level_here, 1, 0)
-    return (gate_row * attended.astype(F32)).astype(BF16)
 
 
 def solution(mesh):

time: 126 us -> 109 us (0.87)
  the two profiles are of different devices: /device:TPU:0 before, /device:TPU:1 now
where the time goes in v2:
time: 109 us
  Pallas kernels  106 us (97%)
  local copies, waits for them, and re-layouts  2.65 us (2%)
    pallas_call x1, Pallas kernels, attention(): pl.pallas_call(functools.partial(kernel, slots, depth), out_shape=jax.Sha...  106 us
    unnamed x1, local copies, waits for them, and re-layouts  2.65 us

profile of v2, /device:TPU:1, one launch (start us, length us, event | category | flops | bytes accessed | tf_op | source)
XLA Modules:
  0.0 108.7 jit_solution(15752685018048578917)
XLA Ops:
  0.0 106.0 %shard_map.91 = bf16[256,3072]{1,0:T(8,128)(2,1)} custom-call(s32[32]{0:T(128)} %levels_hbm.1, s32[32]{0:T(128)} %lengths_hbm.1, s32[32]{0:T(128)} %context_hbm.1, f32[1,128]{1,0:T(1,128)} %bitcast.2, f32[1,128]{1,0:T(1,128)} %bitcast.3, f32[16,3072]{1,0:T(8,128)} %gate_hbm.1, bf16[256,3072]{1,0:T(8,128)(2,1)} %q_hbm.1, bf16[256,3072]{1,0:T(8,128)(2,1)} %k_hbm.1, ...), custom_call_target="tpu_custom_call" | custom-call | flops 12884901888 | bytes 6291456 | tf_op jit(solution)/shard_map/pallas_call | solution.py:345
  106.0 2.7 %copy.11 = bf16[256,3072]{1,0:T(8,128)(2,1)} copy(bf16[256,3072]{1,0:T(8,128)(2,1)} %shard_map.91) | data formatting | bytes 3145728
